TPU v7x, 128 devices: a whole 4x4x4 slice. The times are simulated.
128 devices in a mesh: chan: 64 (over y, x, z_hi, core), win: 2 (over z_lo).
Axes of the slice: x: 4, y: 4, z: 4 (z_hi: 2, z_lo: 2; z = z_hi * 2 + z_lo), core: 2. Of those that a mesh axis runs over, the one named last changes fastest.
Arguments:
- signal: bfloat16 [2048, 256, 1024], P('chan', 'win'), may hold values from -6 to 6
- valid: int32 [2048, 256], P('chan', 'win'), may hold values 0 or 1
- owners: int32 [3], replicated, may hold values from 0 to 63
Outputs:
- cross: bfloat16 [2, 3, 192, 2048, 32], P(None, None, 'win', 'chan')
Inputs may be any that keep to these rules, and one draw needn't show every extreme that they name: owners[s] names an index of chan; steps may repeat a block.
All inputs are finite; a program needn't handle non-finite values. No bound on the sum of `valid` on one device may be relied on, other than what follows from the above.
Results may differ from a plain program's by a relative error of at most 0.0066.
Values may be sent and summed in bfloat16 or wider, within the bound.
No kernel may reach another device: no remote copies, remote signals or barrier semaphores. Data moves between devices by JAX's collectives and lax.ppermute only.
A program may use at most 128 MiB of HBM per device.

v0:
```python
import math

import jax
import jax.numpy as jnp
from jax import lax
from jax.sharding import PartitionSpec as P

SAMPLES = 1024
BINS = 192
FIRST_BIN = 32
WINDOWS = 256
STEPS = 3


def broadcast(x, axis, root):
    mine = lax.axis_index(axis) == root
    return lax.psum(jnp.where(mine, x, jnp.zeros_like(x)), axis)


def band_table(samples, bins, first):
    times = jnp.arange(samples, dtype=jnp.int32)
    freqs = first + jnp.arange(bins, dtype=jnp.int32)
    phase = (freqs[:, None] * times[None, :] % samples).astype(jnp.float32) * (
        2.0 * math.pi / samples
    )
    taper = 0.5 - 0.5 * jnp.cos(times.astype(jnp.float32) * (2.0 * math.pi / samples))
    rows = jnp.concatenate(
        [jnp.cos(phase) * taper[None, :], -jnp.sin(phase) * taper[None, :]], axis=0
    )
    return rows.astype(jnp.bfloat16)


def whiten(table, samples_block, valid_block):
    count, windows, samples = samples_block.shape
    flat = samples_block.reshape(count * windows, samples)
    spec = lax.dot_general(
        table, flat, (((1,), (1,)), ((), ())), preferred_element_type=jnp.float32
    )
    spec = spec.reshape(2, table.shape[0] // 2, count, windows)
    power = jnp.mean(spec[0] * spec[0] + spec[1] * spec[1], axis=0)
    factor = lax.rsqrt(power + 1e-06) * valid_block.astype(jnp.float32)
    return (spec * factor[None, None]).astype(jnp.bfloat16)


def bin_product(left, right):
    return jnp.einsum("fcw,fdw->fcd", left, right, preferred_element_type=jnp.float32)


def local_cross(mine, block):
    real = bin_product(mine[0], block[0]) + bin_product(mine[1], block[1])
    imag = bin_product(mine[1], block[0]) - bin_product(mine[0], block[1])
    return jnp.stack([real, imag])


def per_device(signal, valid, owners):
    table = band_table(SAMPLES, BINS, FIRST_BIN)
    white = whiten(table, signal, valid)
    factor = 1.0 / math.sqrt(WINDOWS)
    results = []
    for step in range(STEPS):
        block = broadcast(white, "chan", owners[step])
        partial_value = local_cross(white, block)
        summed = lax.psum_scatter(partial_value, "win", scatter_dimension=1, tiled=True)
        results.append(summed * factor)
    return jnp.stack(results, axis=1).astype(jnp.bfloat16)


def solution(mesh):
    in_specs = (P("chan", "win", None), P("chan", "win"), P())
    out_specs = P(None, None, "win", "chan", None)
    return jax.shard_map(
        per_device, mesh=mesh, in_specs=in_specs, out_specs=out_specs, check_vma=False
    )
```

profile of v0, /device:TPU:1, one launch (start us, length us, event | category | flops | bytes accessed | tf_op | source)
XLA Modules:
  0.0 819.3 jit_solution(13627539814003357498)
XLA Ops:
  6.5 0.0 all-reduce.3.cloned.1.call-start
  6.6 1.4 fusion.27
  9.9 3.6 multiply_convert_fusion.1
  13.5 5.9 fusion.18
  19.4 0.6 fusion.2
  19.9 0.0 copy-start.3
  19.9 1.3 copy.26
  21.3 2.8 broadcast_select_fusion.2
  24.1 3.0 broadcast_select_fusion.1
  27.1 0.0 all-reduce.3.cloned.1.call-update
  27.1 0.0 reduce-scatter.14.cloned.1.call-start
  27.1 668.1 %all-reduce.3.cloned.1.call-done = (bf16[2,192,32,128]{3,2,1,0:T(8,128)(2,1)}, bf16[2,192,32,128]{3,2,1,0:T(8,128)(2,1)}, bf16[2,192,32,128]{3,2,1,0:T(8,128)(2,1)}) async-done(((bf16[2,192,32,128]{3,2,1,0:T(8,128)(2,1)}, bf16[2,192,32,128]{3,2,1,0:T(8,128)(2,1)}, bf16[2,192,32,128]{3,2,1,0:T(8,128)(2,1)}), (bf16[2,192,32,128]{3,2,1,0:T(8,128)(2,1)}, bf16[2,192,32,128]{3,2,1,0:T(8,128)(2,1)}, ...) | async-done | bytes 9437200 | tf_op jit(solution)/shard_map/psum | solution.py:17
  695.2 2.5 fusion.13
  697.7 0.9 fusion.14
  698.6 1.0 subtract_bitcast_fusion
  699.6 0.9 add_bitcast_fusion
  700.5 3.4 copy_bitcast_fusion
  704.0 5.9 reshape.35
  709.9 0.0 reduce-scatter.14.cloned.1.call-update
  709.9 0.2 reduce-scatter.12.cloned.1.call-start
  710.2 2.5 fusion.11
  712.7 0.9 fusion.12
  713.6 1.0 subtract_bitcast_fusion.1
  714.5 0.9 add_bitcast_fusion.1
  715.5 3.4 copy_bitcast_fusion.1
  718.9 6.3 reshape.33
  725.2 0.0 reduce-scatter.12.cloned.1.call-update
  725.3 0.0 reduce-scatter.10.cloned.1.call-start
  725.3 2.5 fusion.9
  727.8 0.9 fusion.10
  728.8 1.0 subtract_bitcast_fusion.2
  729.7 0.9 add_bitcast_fusion.2
  730.7 3.4 copy_bitcast_fusion.2
  734.1 5.9 reshape.31
  740.0 0.0 reduce-scatter.10.cloned.1.call-update
  740.0 0.0 reduce-scatter.14.cloned.1.call-done
  740.1 2.1 reshape.36
  742.2 1.5 fusion.8
  743.7 3.4 copy.19
  747.1 24.8 %reduce-scatter.12.cloned.1.call-done = f32[96,2048]{1,0:T(8,128)} async-done(((f32[192,2048]{1,0:T(8,128)}), f32[96,2048]{1,0:T(8,128)}) %reduce-scatter.12.cloned.1.call-update) | async-done | bytes 786448
  771.9 2.1 reshape.34
  774.0 1.5 fusion.7
  775.5 3.3 copy.18
  778.8 24.9 %reduce-scatter.10.cloned.1.call-done = f32[96,2048]{1,0:T(8,128)} async-done(((f32[192,2048]{1,0:T(8,128)}), f32[96,2048]{1,0:T(8,128)}) %reduce-scatter.10.cloned.1.call-update) | async-done | bytes 786448
  803.7 2.1 reshape.32
  805.8 1.5 fusion.6
  807.4 2.7 copy.17
  810.0 2.7 pad_maximum_fusion.3
  (10 shorter events, 0.1 us)
Async XLA Ops:
  6.5 688.7 %all-reduce.3.cloned.1.call-start = ((), (), s32[]{:S(2)}) async-start(), calls=%async_computation.6 | async-start | bytes 18874368 | tf_op jit(solution)/shard_map/psum | solution.py:17
  19.9 1.3 copy-start.3
  27.1 713.0 %reduce-scatter.14.cloned.1.call-start = ((), (), s32[]{:S(2)}) async-start(), calls=%async_computation.5 | async-start | bytes 2359296
  695.2 2.5 copy-start.2
  709.9 61.9 %reduce-scatter.12.cloned.1.call-start = ((), (), s32[]{:S(2)}) async-start(), calls=%async_computation.4 | async-start | bytes 2359296
  710.2 2.5 copy-start.1
  725.3 78.5 %reduce-scatter.10.cloned.1.call-start = ((), (), s32[]{:S(2)}) async-start(), calls=%async_computation.3 | async-start | bytes 2359296
  725.3 2.5 copy-start
Sparse Core Ops, SparseCore 0:
  27.2 667.9 all-reduce.2
  710.0 29.6 reduce-scatter.13
  742.2 29.6 reduce-scatter.11
  774.1 29.6 reduce-scatter.9
where the time goes:
time: 820 us; the launch traced here: 819 us
  waiting for transfers between devices  718 us (88%)
  local copies, waits for them, and re-layouts  36.5 us (4%)
  other arithmetic  27.6 us (3%)
  matrix products  21.8 us (3%)
  between operations  15.2 us (2%)
    psum x1, waiting for transfers between devices, broadcast(): return lax.psum(jnp.where(mine, x, jnp.zeros_like(x)), axis)  668 us
    unnamed x7, waiting for transfers between devices  49.8 us
    unnamed x15, local copies, waits for them, and re-layouts  25.7 us
  transfers between devices with their start and end apart: 4, of which 3 were waited for; matrix products, arithmetic and copies ran while one was open for 5% of the time, Pallas kernels for 0%

commit v1 on v0

--- a/solution.py
+++ b/solution.py
@@ -10,11 +10,8 @@
 FIRST_BIN = 32
 WINDOWS = 256
 STEPS = 3
-
-
-def broadcast(x, axis, root):
-    mine = lax.axis_index(axis) == root
-    return lax.psum(jnp.where(mine, x, jnp.zeros_like(x)), axis)
+CH_DEV = 32
+N_CHAN = 64
 
 
 def band_table(samples, bins, first):
@@ -42,27 +39,43 @@
     return (spec * factor[None, None]).astype(jnp.bfloat16)
 
 
-def bin_product(left, right):
-    return jnp.einsum("fcw,fdw->fcd", left, right, preferred_element_type=jnp.float32)
+def by_destination(white):
+    parts = white.reshape(2, 2, 3, 32, CH_DEV, 128)
+    full = jnp.stack([parts[:, :, 0], parts[:, :, 2]], axis=0)
+    full = jnp.transpose(full, (3, 0, 2, 1, 4, 5))
+    mid = parts[:, :, 1].reshape(2, 2, 32, 2, 16, 128)
+    mid = jnp.transpose(mid, (2, 3, 1, 0, 4, 5))
+    return jnp.concatenate([full, mid], axis=4).reshape(128, 2, 48, 128)
 
 
-def local_cross(mine, block):
-    real = bin_product(mine[0], block[0]) + bin_product(mine[1], block[1])
-    imag = bin_product(mine[1], block[0]) - bin_product(mine[0], block[1])
-    return jnp.stack([real, imag])
+def against(left, block):
+    swapped = jnp.stack([-block[:, :, 1], block[:, :, 0]], axis=2)
+    both = jnp.stack([block, swapped])
+    return jnp.einsum("iwrct,qswrjt->icqsj", left, both, preferred_element_type=jnp.float32)
 
 
 def per_device(signal, valid, owners):
     table = band_table(SAMPLES, BINS, FIRST_BIN)
     white = whiten(table, signal, valid)
-    factor = 1.0 / math.sqrt(WINDOWS)
-    results = []
-    for step in range(STEPS):
-        block = broadcast(white, "chan", owners[step])
-        partial_value = local_cross(white, block)
-        summed = lax.psum_scatter(partial_value, "win", scatter_dimension=1, tiled=True)
-        results.append(summed * factor)
-    return jnp.stack(results, axis=1).astype(jnp.bfloat16)
+    got = lax.all_to_all(by_destination(white), ("chan", "win"), 0, 0, tiled=True)
+    got = got.reshape(N_CHAN, 2, 2, 48, 128)
+    planned = jnp.stack([lax.dynamic_index_in_dim(got, owners[s], 0, False) for s in range(STEPS)])
+    own = planned[:, :, :, 32:]
+    other = lax.ppermute(own, "chan", [(i, i ^ 1) for i in range(N_CHAN)])
+    first = (lax.axis_index("chan") & 1) == 0
+    mid_block = jnp.where(
+        first, jnp.concatenate([own, other], axis=3), jnp.concatenate([other, own], axis=3)
+    )
+    full = against(got[:, :, :, :32], planned[:, :, :, :32])
+    mid = against(got[:, :, :, 32:], mid_block)
+    result = jnp.concatenate([full, mid], axis=1) * (1.0 / math.sqrt(WINDOWS))
+    result = result.astype(jnp.bfloat16).reshape(N_CHAN, 72, 128)
+    back = lax.all_to_all(result, "chan", 0, 0, tiled=True)
+    back = back.reshape(32, 2, 48, 2, STEPS, 32)
+    low, high = back[:, 0, :32], back[:, 1, :32]
+    middle = jnp.concatenate([back[:, 0, 32:], back[:, 1, 32:]], axis=1)
+    out = jnp.stack([low, middle, high])
+    return jnp.transpose(out, (3, 4, 0, 1, 2, 5)).reshape(2, STEPS, 96, 32, 32)
 
 
 def solution(mesh):

time: 820 us -> 142 us (0.17)
  waiting for transfers between devices: 718 us -> 35.1 us
  blocking collectives: 0 us -> 24.9 us
  starting transfers between devices: 0.31 us -> 12.7 us
  matrix products: 21.8 us -> 10.2 us
  between operations: 15.2 us -> 6 us
    psum x1 -> x0, waiting for transfers between devices: 668 us -> none  [broadcast(): return lax.psum(jnp.where(mine, x, jnp.zeros_like(x)), axis)]
    unnamed x7 -> x0, waiting for transfers between devices: 49.8 us -> none
    all_to_all x0 -> x1, waiting for transfers between devices: none -> 35.1 us  [per_device(): lax.all_to_all(by_destination(white), ('chan', 'win'), 0, 0, tiled=True)]
    all_to_all x0 -> x1, blocking collectives: none -> 24.9 us  [per_device(): back = lax.all_to_all(result, 'chan', 0, 0, tiled=True)]
    unnamed x15 -> x6, local copies, waits for them, and re-layouts: 25.7 us -> 1.31 us
    reshape x0 -> x2, local copies, waits for them, and re-layouts: none -> 15.3 us  [the longest x1 8.53 us: per_device(): return jnp.transpose(out, (3, 4, 0, 1, 2, 5)).reshape(2, STEPS, 96, 32, 32)]
    dot_general x12 -> x2, matrix products: 16 us -> 4.28 us  [against(): jnp.einsum('iwrct,qswrjt->icqsj', left, both, preferred_element_type=jnp....]
    all_to_all x0 -> x1, starting transfers between devices: none -> 11.5 us  [per_device(): lax.all_to_all(by_destination(white), ('chan', 'win'), 0, 0, tiled=True)]
  transfers between devices with their start and end apart: 4 -> 2, of which waited for: 3 -> 1; matrix products, arithmetic and copies ran while one was open for 5% -> 3% of each run, Pallas kernels for 0% -> 0%
where the time goes in v1:
time: 142 us; the launch traced here: 141 us
  waiting for transfers between devices  35.1 us (25%)
  local copies, waits for them, and re-layouts  29.6 us (21%)
  blocking collectives  24.9 us (18%)
  other arithmetic  22.7 us (16%)
  starting transfers between devices  12.7 us (9%)
  matrix products  10.2 us (7%)
  between operations  6 us (4%)
    all_to_all x1, waiting for transfers between devices, per_device(): lax.all_to_all(by_destination(white), ('chan', 'win'), 0, 0, tiled=True)  35.1 us
    all_to_all x1, blocking collectives, per_device(): back = lax.all_to_all(result, 'chan', 0, 0, tiled=True)  24.9 us
    another operation x2, other arithmetic, per_device(): out = jnp.stack([low, middle, high])  16.1 us
    all_to_all x1, starting transfers between devices, per_device(): lax.all_to_all(by_destination(white), ('chan', 'win'), 0, 0, tiled=True)  11.5 us
    reshape x1, local copies, waits for them, and re-layouts, per_device(): return jnp.transpose(out, (3, 4, 0, 1, 2, 5)).reshape(2, STEPS, 96, 32, 32)  8.53 us
    reshape x1, local copies, waits for them, and re-layouts, per_device(): back = back.reshape(32, 2, 48, 2, STEPS, 32)  6.78 us
    dot_general x1, matrix products, whiten(): lax.dot_general(table, flat, (((1,), (1,)), ((), ())), preferred_element_...  5.88 us
    dot_general x2, matrix products, against(): jnp.einsum('iwrct,qswrjt->icqsj', left, both, preferred_element_type=jnp....  4.28 us
  transfers between devices with their start and end apart: 2, of which 1 were waited for; matrix products, arithmetic and copies ran while one was open for 3% of the time, Pallas kernels for 0%

profile of v1, /device:TPU:1, one launch (start us, length us, event | category | flops | bytes accessed | tf_op | source)
XLA Modules:
  0.0 141.2 jit_solution(17687478077462974836)
XLA Ops:
  0.1 3.6 %multiply_convert_fusion.1 = (bf16[192,1024]{1,0:T(8,128)(2,1)S(1)}, bf16[192,1024]{1,0:T(8,128)(2,1)S(1)}) fusion(f32[1024]{0:T(1024)S(1)} %multiply_subtract_fusion, s32[192]{0:T(256)S(1)} %iota_add_fusion), kind=kLoop, calls=%fused_computation.36 | loop fusion | flops 3735552 | bytes 791296 | tf_op jit(solution)/shard_map/convert
  3.6 5.9 %fusion.13 = f32[384,4096]{1,0:T(8,128)S(1)} fusion(bf16[4096,1024]{1,0:T(8,128)(2,1)} %bitcast.78, bf16[192,1024]{1,0:T(8,128)(2,1)S(1)} %get-tuple-element.20, bf16[192,1024]{1,0:T(8,128)(2,1)S(1)} %get-tuple-element.19), kind=kOutput, calls=%fused_computation.31 | convolution fusion | flops 3222798336 | bytes 15466496 | tf_op jit(solution)/shard_map/dot_general | solution.py:33
  9.5 0.6 fusion.3
  10.1 0.0 copy-start
  10.1 1.3 copy.92
  11.4 0.0 copy-done
  11.4 0.8 fusion
  12.3 0.6 slice_bitcast_fusion.5
  12.9 0.2 maximum_bitcast_fusion
  13.1 0.6 pad_maximum_fusion.1
  13.7 2.5 %copy.58 = bf16[32,2,2,2,48,128]{5,4,3,2,1,0:T(8,128)(2,1)} copy(bf16[32,2,2,2,48,128]{5,4,0,2,3,1:T(8,128)(2,1)S(1)} %pad_maximum_fusion.1) | data formatting | bytes 6291456 | tf_op jit(solution)/shard_map/concatenate | solution.py:48
  16.2 0.0 copy-start.1
  16.2 11.5 %all-to-all-start = ((bf16[128,2,48,128]{3,2,1,0:T(8,128)(2,1)}), bf16[128,2,48,128]{3,2,1,0:T(8,128)(2,1)S(1)}, u32[]{:S(2)}, u32[]{:S(2)}) async-start(bf16[128,2,48,128]{3,2,1,0:T(8,128)(2,1)} %bitcast.74), calls=%async_computation | async-start | bytes 6291456 | tf_op jit(solution)/shard_map/all_to_all | solution.py:60
  27.7 0.0 copy-done.1
  27.7 0.6 fusion.28
  34.1 35.1 %all-to-all-done = bf16[128,2,48,128]{3,2,1,0:T(8,128)(2,1)S(1)} async-done(((bf16[128,2,48,128]{3,2,1,0:T(8,128)(2,1)}), bf16[128,2,48,128]{3,2,1,0:T(8,128)(2,1)S(1)}, u32[]{:S(2)}, u32[]{:S(2)}) %all-to-all-start) | async-done | bytes 3145760 | tf_op jit(solution)/shard_map/all_to_all | solution.py:60
  69.3 0.5 copy_bitcast_fusion
  69.9 1.2 collective-permute-start
  71.1 2.8 %fusion.6 = f32[64,32,2,3,32]{0,4,3,2,1:T(8,128)S(1)} fusion(bf16[64,2,2,32,128,1,1]{4,3,1,2,0,5,6:T(8,128)(2,1)S(1)} %copy_bitcast_fusion, bf16[1,3,2,2,32,128]{5,4,2,3,1,0:T(8,128)(2,1)S(1)} %get-tuple-element.24, bf16[1,3,2,2,32,128]{5,4,2,3,1,0:T(8,128)(2,1)S(1)} %get-tuple-element.25), kind=kOutput, calls=%fused_computation.17 | convolution fusion | flops 403046400 | bytes 3866624 | tf_op jit(solution)/shard_map/iwrct,qswrjt->icqsj/dot_general | solution.py:54
  73.9 0.2 copy_bitcast_fusion.1
  74.1 0.0 collective-permute-done
  74.3 1.5 %convolution_bitcast_fusion = f32[64,16,2,3,32]{0,4,3,2,1:T(8,128)S(1)} fusion(bf16[64,2,2,16,128,1,1]{4,3,1,2,0,5,6:T(8,128)(2,1)S(1)} %copy_bitcast_fusion.1, bf16[1,3,2,2,32,128]{5,4,2,3,1,0:T(8,128)(2,1)S(1)} %maximum_bitcast_fusion.7, bf16[1,3,2,2,32,128]{5,4,2,3,1,0:T(8,128)(2,1)S(1)} %maximum_select_fusion), kind=kOutput, calls=%fused_computation.18 | convolution fusion | flops 201719808 | bytes 2031616 | tf_op jit(solution)/shard_map/iwrct,qswrjt->icqsj/dot_general | solution.py:54
  75.7 0.7 fusion.1
  76.5 1.2 copy.66
  77.7 24.9 %all_to_all.10 = bf16[64,72,128]{2,1,0:T(8,128)(2,1)S(1)} all-to-all(bf16[64,72,128]{2,1,0:T(8,128)(2,1)S(1)} %copy.66), channel_id=1, replica_groups=mesh['chan'=64,'win'=2] {'chan'}, dimensions={0} | all-to-all | bytes 2359296 | tf_op jit(solution)/shard_map/all_to_all | solution.py:73
  102.5 6.8 %reshape.107 = bf16[32,2,48,2,3,32]{5,4,3,2,1,0:T(4,128)(2,1)} reshape(bf16[64,72,128]{2,1,0:T(8,128)(2,1)S(1)} %all_to_all.10) | data formatting | bytes 2359296 | tf_op jit(solution)/shard_map/reshape | solution.py:74
  109.3 3.1 %slice_bitcast_fusion.3 = (bf16[32,16,2,3,32]{4,3,2,1,0:T(4,128)(2,1)S(1)}, bf16[32,16,2,3,32]{4,3,2,1,0:T(4,128)(2,1)S(1)}) fusion(bf16[32,2,48,2,3,32]{5,4,3,2,1,0:T(4,128)(2,1)} %reshape.107), kind=kLoop, calls=%fused_computation.23 | loop fusion | bytes 786432 | tf_op jit(solution)/shard_map/squeeze | solution.py:76
  112.4 4.1 %slice_bitcast_fusion.1 = (bf16[1,32,32,2,3,32]{5,4,3,2,1,0:T(4,128)(2,1)S(1)}, bf16[1,32,32,2,3,32]{5,4,3,2,1,0:T(4,128)(2,1)S(1)}) fusion(bf16[32,2,48,2,3,32]{5,4,3,2,1,0:T(4,128)(2,1)} %reshape.107), kind=kLoop, calls=%fused_computation.11 | loop fusion | bytes 1572864 | tf_op jit(solution)/shard_map/stack;squeeze | solution.py:77
  116.5 1.6 %maximum_bitcast_fusion.1 = bf16[1,32,32,2,3,32]{5,4,3,2,1,0:T(4,128)(2,1)S(1)} fusion(bf16[32,16,2,3,32]{4,3,2,1,0:T(4,128)(2,1)S(1)} %get-tuple-element.8, bf16[32,16,2,3,32]{4,3,2,1,0:T(4,128)(2,1)S(1)} %get-tuple-element.7), kind=kLoop, calls=%fused_computation.13 | loop fusion | flops 196608 | bytes 786432 | tf_op jit(solution)/shard_map/stack | solution.py:77
  118.2 14.5 %pad_maximum_fusion = bf16[3,32,32,2,3,32]{5,4,3,2,1,0:T(4,128)(2,1)} fusion(bf16[1,32,32,2,3,32]{5,4,3,2,1,0:T(4,128)(2,1)S(1)} %get-tuple-element.6, bf16[1,32,32,2,3,32]{5,4,3,2,1,0:T(4,128)(2,1)S(1)} %maximum_bitcast_fusion.1, bf16[1,32,32,2,3,32]{5,4,3,2,1,0:T(4,128)(2,1)S(1)} %get-tuple-element.5), kind=kLoop, calls=%fused_computation | loop fusion | flops 1179648 | bytes 2359296 | tf_op jit(solution)/shard_map/stack | solution.py:77
  132.7 8.5 %copy.79 = bf16[2,3,96,32,32]{2,4,3,1,0:T(8,128)(2,1)} copy(bf16[2,3,96,32,32]{4,1,0,3,2:T(4,128)(2,1)} %bitcast.70) | data formatting | bytes 2359296 | tf_op jit(solution)/shard_map/reshape | solution.py:78
  (13 shorter events, 0.2 us)
Async XLA Ops:
  10.1 1.3 copy-start
  16.2 11.5 %copy-start.1 = (s32[3]{0:T(128)S(1)}, s32[3]{0:T(128)}, u32[]{:S(2)}) copy-start(s32[3]{0:T(128)} %param.5) | copy-start | bytes 40
  16.2 53.0 %all-to-all-start = ((bf16[128,2,48,128]{3,2,1,0:T(8,128)(2,1)}), bf16[128,2,48,128]{3,2,1,0:T(8,128)(2,1)S(1)}, u32[]{:S(2)}, u32[]{:S(2)}) async-start(bf16[128,2,48,128]{3,2,1,0:T(8,128)(2,1)} %bitcast.74), calls=%async_computation | async-start | bytes 6291456 | tf_op jit(solution)/shard_map/all_to_all | solution.py:60
  69.9 4.3 %collective-permute-start = (bf16[3,2,2,16,128]{4,3,1,2,0:T(8,128)(2,1)S(1)}, bf16[3,2,2,16,128]{4,3,1,2,0:T(8,128)(2,1)S(1)}, u32[]{:S(2)}, u32[]{:S(2)}) collective-permute-start(bf16[3,2,2,16,128]{4,3,1,2,0:T(8,128)(2,1)S(1)} %get-tuple-element.18), channel_id=1, source_target_pairs={{0,2},{2,0},{4,6},{6,4},{8,10},{10,8},{12,14},{14,12},{16,18},{18,... | collective-permute-start | bytes 147464 | tf_op jit(solution)/shard_map/ppermute | solution.py:64

commit v2 on v0

v2 whole, which is shorter than its diff:
```python
import math

import jax
import jax.numpy as jnp
from jax import lax
from jax.experimental import pallas as pl
from jax.experimental.pallas import tpu as pltpu
from jax.sharding import PartitionSpec as P

SAMPLES = 1024
BINS = 192
WINDOWS = 256
STEPS = 3
CH_DEV = 32
N_CHAN = 64
LANES = 128
COLUMNS = 2 * STEPS * CH_DEV
FULL_ROWS, ROWS = 48, 72


def vmem():
    return pl.BlockSpec(memory_space=pltpu.VMEM)


def limit(mib):
    return pltpu.CompilerParams(vmem_limit_bytes=mib << 20)


def angles(rows, scale):
    times = lax.broadcasted_iota(jnp.int32, (rows, SAMPLES), 1)
    freqs = lax.broadcasted_iota(jnp.int32, (rows, SAMPLES), 0) * scale
    return (freqs * times % SAMPLES).astype(jnp.float32) * (2.0 * math.pi / SAMPLES)


def fill_table(table):
    fine = angles(32, 1)
    coarse = angles(8, 32)
    times = lax.broadcasted_iota(jnp.int32, (1, SAMPLES), 1).astype(jnp.float32)
    taper = 0.5 - 0.5 * jnp.cos(times * (2.0 * math.pi / SAMPLES))
    fine_cos, fine_sin = jnp.cos(fine) * taper, jnp.sin(fine) * taper
    coarse_cos, coarse_sin = jnp.cos(coarse), jnp.sin(coarse)
    for a in range(6):
        cos_a, sin_a = coarse_cos[a + 1 : a + 2], coarse_sin[a + 1 : a + 2]
        real = cos_a * fine_cos - sin_a * fine_sin
        imag = -sin_a * fine_cos - cos_a * fine_sin
        table[32 * a : 32 * a + 32, :] = real.astype(jnp.bfloat16)
        table[BINS + 32 * a : BINS + 32 * a + 32, :] = imag.astype(jnp.bfloat16)


def whiten_kernel(signal, valid, out, table, white):
    g = pl.program_id(0)

    @pl.when(g == 0)
    def _():
        fill_table(table)

    weights = valid[...].astype(jnp.float32)
    for pair in range(8):
        both = signal[2 * pair : 2 * pair + 2].reshape(2 * LANES, SAMPLES)
        spec = lax.dot_general(
            table[...], both, (((1,), (1,)), ((), ())), preferred_element_type=jnp.float32
        )
        power = jnp.sum(spec * spec, axis=0, keepdims=True) * (1.0 / BINS)
        factor = lax.rsqrt(power + 1e-06)
        for one in range(2):
            c = 2 * pair + one
            lanes = slice(one * LANES, (one + 1) * LANES)
            scale = factor[:, lanes] * weights[c : c + 1, :]
            white[c] = (spec[:, lanes] * scale).astype(jnp.bfloat16)
    own_rows = pl.ds(pl.multiple_of(16 * g, 16), 16)
    for h in range(2):
        for r in range(2):
            for m in range(3):
                start = BINS * r + 96 * h + 32 * m
                rows = jnp.swapaxes(white[:, start : start + 32, :], 0, 1)
                if m == 2:
                    out[:, g, h, r, 32:48, :] = rows
                else:
                    out[16 * m : 16 * m + 16, :, h, r, own_rows, :] = rows.reshape(16, 2, 16, LANES)


def whitened(signal, valid):
    return pl.pallas_call(
        whiten_kernel,
        grid=(2,),
        in_specs=[
            pl.BlockSpec((16, LANES, SAMPLES), lambda g: (g, 0, 0)),
            pl.BlockSpec((16, LANES), lambda g: (g, 0)),
        ],
        out_specs=vmem(),
        out_shape=jax.ShapeDtypeStruct((32, 2, 2, 2, 48, LANES), jnp.bfloat16),
        scratch_shapes=[
            pltpu.VMEM((2 * BINS, SAMPLES), jnp.bfloat16),
            pltpu.VMEM((16, 2 * BINS, LANES), jnp.bfloat16),
        ],
        compiler_params=limit(54),
        cost_estimate=pl.CostEstimate(
            flops=2 * 2 * BINS * SAMPLES * 4096, bytes_accessed=12 << 20, transcendentals=0
        ),
        name="whiten",
    )(signal, valid)


def pick_kernel(owners, got, out):
    for s in range(STEPS):
        out[s] = got[owners[s], :, :, 32:48, :]


def picked(owners, got):
    return pl.pallas_call(
        pick_kernel,
        in_specs=[pl.BlockSpec(memory_space=pltpu.SMEM), vmem()],
        out_specs=vmem(),
        out_shape=jax.ShapeDtypeStruct((STEPS, 2, 2, 16, LANES), jnp.bfloat16),
        compiler_params=limit(16),
        cost_estimate=pl.CostEstimate(flops=0, bytes_accessed=98304, transcendentals=0),
        name="pick",
    )(owners, got)


def planned_columns(planned):
    real = [jnp.concatenate([b[0, 0], b[0, 1], b[1, 0], b[1, 1]], axis=1) for b in planned]
    imag = [jnp.concatenate([-b[0, 1], b[0, 0], -b[1, 1], b[1, 0]], axis=1) for b in planned]
    return jnp.concatenate(real + imag, axis=0)


def products(left, columns):
    count, channels = left.shape[0], left.shape[3]
    rows = jnp.concatenate(
        [left[:, w, r].reshape(count * channels, LANES) for w in range(2) for r in range(2)], axis=1
    )
    result = lax.dot_general(
        rows, columns, (((1,), (1,)), ((), ())), preferred_element_type=jnp.float32
    )
    return (result * (1.0 / math.sqrt(WINDOWS))).reshape(count, channels, COLUMNS)


def packed(result):
    rest = result[:, :, LANES:]
    parts = [result[:, :, :LANES]]
    for start in range(0, result.shape[1], 16):
        parts.append(
            jnp.concatenate([rest[:, start : start + 8], rest[:, start + 8 : start + 16]], axis=2)
        )
    return jnp.concatenate(parts, axis=1).astype(jnp.bfloat16)


def full_kernel(owners, got, out, columns):
    columns[...] = planned_columns([got[owners[s], :, :, :32, :] for s in range(STEPS)])
    for start in range(0, N_CHAN, 8):
        left = got[start : start + 8, :, :, :32, :]
        out[start : start + 8, :FULL_ROWS, :] = packed(products(left, columns[...]))


def cross_full(owners, got):
    return pl.pallas_call(
        full_kernel,
        in_specs=[pl.BlockSpec(memory_space=pltpu.SMEM), vmem()],
        out_specs=vmem(),
        out_shape=jax.ShapeDtypeStruct((N_CHAN, ROWS, LANES), jnp.bfloat16),
        scratch_shapes=[pltpu.VMEM((COLUMNS, 4 * LANES), jnp.bfloat16)],
        compiler_params=limit(16),
        cost_estimate=pl.CostEstimate(
            flops=2 * 2048 * 512 * 192, bytes_accessed=3 << 20, transcendentals=0
        ),
        name="cross_full",
    )(owners, got)


def mid_kernel(core, got, own, other, partial, out, columns):
    del partial
    first = core[0] == 0
    planned = []
    for s in range(STEPS):
        mine, theirs = own[s], other[s]
        low, high = jnp.where(first, mine, theirs), jnp.where(first, theirs, mine)
        planned.append(jnp.concatenate([low, high], axis=2))
    columns[...] = planned_columns(planned)
    for start in range(0, N_CHAN, 16):
        left = got[start : start + 16, :, :, 32:48, :]
        out[start : start + 16, FULL_ROWS:, :] = packed(products(left, columns[...]))


def cross_mid(core, got, own, other, partial):
    return pl.pallas_call(
        mid_kernel,
        in_specs=[pl.BlockSpec(memory_space=pltpu.SMEM)] + [vmem()] * 4,
        out_specs=vmem(),
        out_shape=jax.ShapeDtypeStruct((N_CHAN, ROWS, LANES), jnp.bfloat16),
        scratch_shapes=[pltpu.VMEM((COLUMNS, 4 * LANES), jnp.bfloat16)],
        input_output_aliases={4: 0},
        compiler_params=limit(16),
        cost_estimate=pl.CostEstimate(
            flops=2 * 1024 * 512 * 192, bytes_accessed=2 << 20, transcendentals=0
        ),
        name="cross_mid",
    )(core, got, own, other, partial)


def order_kernel(back, out):
    g = pl.program_id(0)
    first = pl.multiple_of(16 * g, 16)

    def turned(full, mid):
        return jnp.concatenate([full, mid], axis=0).T

    full = jnp.swapaxes(back[:, :, pl.ds(first, 16), :].reshape(N_CHAN, 16, LANES), 0, 1)
    mid = jnp.swapaxes(back[:, g, 48:64, :], 0, 1)
    for c in range(16):
        columns = turned(full[c], mid[c])
        for u in range(4):
            out[u // STEPS, u % STEPS, c] = columns[32 * u : 32 * u + 32]
    rest = back[:, :, 32:48, :].reshape(N_CHAN, 16, LANES).astype(jnp.float32)
    rest = jnp.where(g == 0, rest[:, :8], rest[:, 8:])
    rest = jnp.swapaxes(rest, 0, 1).astype(jnp.bfloat16)
    mid = jnp.swapaxes(back[:, g, 64:72, :].astype(jnp.float32), 0, 1).astype(jnp.bfloat16)
    for e in range(8):
        columns = turned(rest[e], mid[e])
        for half in range(2):
            for u in (4, 5):
                start = 64 * half + 32 * (u - 4)
                out[u // STEPS, u % STEPS, e + 8 * half] = columns[start : start + 32]


def ordered(back):
    return pl.pallas_call(
        order_kernel,
        grid=(2,),
        in_specs=[vmem()],
        out_specs=pl.BlockSpec((2, STEPS, 16, 32, 96), lambda g: (0, 0, g, 0, 0)),
        out_shape=jax.ShapeDtypeStruct((2, STEPS, 32, 32, 96), jnp.bfloat16),
        compiler_params=limit(24),
        cost_estimate=pl.CostEstimate(flops=0, bytes_accessed=4 << 20, transcendentals=0),
        name="order",
    )(back.reshape(32, 2, ROWS, LANES))


def per_device(signal, valid, owners):
    got = lax.all_to_all(
        whitened(signal, valid).reshape(128, 2, 48, LANES), ("chan", "win"), 0, 0, tiled=True
    ).reshape(N_CHAN, 2, 2, 48, LANES)
    own = picked(owners, got)
    other = lax.ppermute(own, "chan", [(i, i ^ 1) for i in range(N_CHAN)])
    core = (lax.axis_index("chan") & 1).reshape(1)
    result = cross_mid(core, got, own, other, cross_full(owners, got))
    back = lax.all_to_all(result, "chan", 0, 0, tiled=True)
    return jnp.transpose(ordered(back), (0, 1, 4, 2, 3))


def solution(mesh):
    in_specs = (P("chan", "win", None), P("chan", "win"), P())
    out_specs = P(None, None, "win", "chan", None)
    return jax.shard_map(
        per_device, mesh=mesh, in_specs=in_specs, out_specs=out_specs, check_vma=False
    )
```

time: 820 us -> 93.5 us (0.11)
  waiting for transfers between devices: 718 us -> 0.01 us
  blocking collectives: 0 us -> 77.9 us
  local copies, waits for them, and re-layouts: 36.5 us -> 0.01 us
  other arithmetic: 27.6 us -> 0 us
  matrix products: 21.8 us -> 0 us
  between operations: 15.2 us -> 0.02 us
  Pallas kernels: 0 us -> 14.3 us
    psum x1 -> x0, waiting for transfers between devices: 668 us -> none  [broadcast(): return lax.psum(jnp.where(mine, x, jnp.zeros_like(x)), axis)]
    all_to_all x0 -> x2, blocking collectives: none -> 77.9 us  [the longest x1 53 us: per_device(): lax.all_to_all(whitened(signal, valid).reshape(128, 2, 48, LANES), ('chan...]
    unnamed x7 -> x0, waiting for transfers between devices: 49.8 us -> none
    unnamed x15 -> x2, local copies, waits for them, and re-layouts: 25.7 us -> 0.01 us
    dot_general x13 -> x0, matrix products: 21.8 us -> none  [the longest x12 16 us: bin_product(): jnp.einsum('fcw,fdw->fcd', left, right, preferred_element_type=jnp.float32)]
    pallas_call x0 -> x5, Pallas kernels: none -> 14.3 us  [the longest x1 10.3 us: whitened(): pl.pallas_call(whiten_kernel, grid=(2,), in_specs=[pl.BlockSpec((16, LANE...]
    another operation x5 -> x0, other arithmetic: 10.9 us -> none  [the longest x4 7.3 us: per_device(): return jnp.stack(results, axis=1).astype(jnp.bfloat16)]
    unnamed x3 -> x0, other arithmetic: 10.3 us -> none
  transfers between devices with their start and end apart: 4 -> 1, of which waited for: 3 -> 0; matrix products, arithmetic and copies ran while one was open for 5% -> 0% of each run, Pallas kernels for 0% -> 1%
where the time goes in v2:
time: 93.5 us; the launch traced here: 93.3 us
  blocking collectives  77.9 us (83%)
  Pallas kernels  14.3 us (15%)
  starting transfers between devices  1.06 us (1%)
    all_to_all x1, blocking collectives, per_device(): lax.all_to_all(whitened(signal, valid).reshape(128, 2, 48, LANES), ('chan...  53 us
    all_to_all x1, blocking collectives, per_device(): back = lax.all_to_all(result, 'chan', 0, 0, tiled=True)  24.9 us
    pallas_call x1, Pallas kernels, whitened(): pl.pallas_call(whiten_kernel, grid=(2,), in_specs=[pl.BlockSpec((16, LANE...  10.3 us
  transfers between devices with their start and end apart: 1, of which 0 were waited for; matrix products, arithmetic and copies ran while one was open for 0% of the time, Pallas kernels for 1%

profile of v2, /device:TPU:1, one launch (start us, length us, event | category | flops | bytes accessed | tf_op | source)
XLA Modules:
  0.0 93.3 jit_solution(12460427802107525776)
XLA Ops:
  0.0 10.3 %whiten.1 = bf16[32,2,2,2,48,128]{5,4,3,2,1,0:T(8,128)(2,1)} custom-call(bf16[32,128,1024]{2,1,0:T(8,128)(2,1)} %signal.1, s32[32,128]{1,0:T(8,128)} %valid.1), custom_call_target="tpu_custom_call" | custom-call | flops 3221225472 | bytes 12582912 | tf_op jit(solution)/shard_map/whiten/pallas_call | solution.py:83
  10.3 0.0 copy-start
  10.3 53.0 %all_to_all.10 = bf16[128,2,48,128]{3,2,1,0:T(8,128)(2,1)S(1)} all-to-all(bf16[128,2,48,128]{3,2,1,0:T(8,128)(2,1)} %bitcast.9), channel_id=1, replica_groups=mesh['chan'=64,'win'=2] {'chan','win'}, dimensions={0} | all-to-all | bytes 6291456 | tf_op jit(solution)/shard_map/all_to_all | solution.py:239
  63.3 0.0 copy-done
  63.3 0.5 pick.1.own
  63.9 1.1 %collective-permute-start = (bf16[3,2,2,16,128]{4,3,2,1,0:T(8,128)(2,1)S(1)}, bf16[3,2,2,16,128]{4,3,2,1,0:T(8,128)(2,1)S(1)}, u32[]{:S(2)}, u32[]{:S(2)}) collective-permute-start(bf16[3,2,2,16,128]{4,3,2,1,0:T(8,128)(2,1)S(1)} %pick.1.own), channel_id=1, source_target_pairs={{0,2},{2,0},{4,6},{6,4},{8,10},{10,8},{12,14},{14,12},{16,18},{18,... | collective-permute-start | bytes 147464 | tf_op jit(solution)/shard_map/ppermute | solution.py:243
  64.9 1.3 %cross_full.1.partial = bf16[64,72,128]{2,1,0:T(8,128)(2,1)S(1)} custom-call(s32[3]{0:T(128)S(1)} %copy-done, bf16[64,2,2,48,128]{4,3,2,1,0:T(8,128)(2,1)S(1)} %bitcast.6), custom_call_target="tpu_custom_call" | custom-call | flops 402653184 | bytes 3145728 | tf_op jit(solution)/shard_map/cross_full/pallas_call | solution.py:156
  66.3 0.0 collective-permute-done.other
  66.3 0.5 cross_mid.1
  66.8 24.9 %all_to_all.11 = bf16[64,72,128]{2,1,0:T(8,128)(2,1)S(1)} all-to-all(bf16[64,72,128]{2,1,0:T(8,128)(2,1)S(1)} %cross_mid.1), channel_id=1, replica_groups=mesh['chan'=64,'win'=2] {'chan'}, dimensions={0} | all-to-all | bytes 2359296 | tf_op jit(solution)/shard_map/all_to_all | solution.py:246
  91.7 1.6 %order.1 = bf16[2,3,32,32,96]{4,3,2,1,0:T(8,128)(2,1)} custom-call(bf16[32,2,72,128]{3,2,1,0:T(8,128)(2,1)S(1)} %bitcast.8), custom_call_target="tpu_custom_call" | custom-call | bytes 4194304 | tf_op jit(solution)/shard_map/order/pallas_call | solution.py:226
Async XLA Ops:
  10.3 53.0 %copy-start = (s32[3]{0:T(128)S(1)}, s32[3]{0:T(128)}, u32[]{:S(2)}) copy-start(s32[3]{0:T(128)} %owners.3) | copy-start | bytes 40
  63.9 2.4 %collective-permute-start = (bf16[3,2,2,16,128]{4,3,2,1,0:T(8,128)(2,1)S(1)}, bf16[3,2,2,16,128]{4,3,2,1,0:T(8,128)(2,1)S(1)}, u32[]{:S(2)}, u32[]{:S(2)}) collective-permute-start(bf16[3,2,2,16,128]{4,3,2,1,0:T(8,128)(2,1)S(1)} %pick.1.own), channel_id=1, source_target_pairs={{0,2},{2,0},{4,6},{6,4},{8,10},{10,8},{12,14},{14,12},{16,18},{18,... | collective-permute-start | bytes 147464 | tf_op jit(solution)/shard_map/ppermute | solution.py:243

commit v3 on v2

--- a/solution.py
+++ b/solution.py
@@ -16,6 +16,7 @@
 LANES = 128
 COLUMNS = 2 * STEPS * CH_DEV
 FULL_ROWS, ROWS = 48, 72
+CHUNKS = ((0, 4), (4, 12), (12, 32))
 
 
 def vmem():
@@ -47,58 +48,80 @@
         table[BINS + 32 * a : BINS + 32 * a + 32, :] = imag.astype(jnp.bfloat16)
 
 
-def whiten_kernel(signal, valid, out, table, white):
-    g = pl.program_id(0)
-
-    @pl.when(g == 0)
-    def _():
-        fill_table(table)
-
-    weights = valid[...].astype(jnp.float32)
-    for pair in range(8):
-        both = signal[2 * pair : 2 * pair + 2].reshape(2 * LANES, SAMPLES)
+def whiten_kernel(signal, valid, white, samples, usable, table, sems):
+    copies = [pltpu.make_async_copy(valid, usable, sems.at[len(CHUNKS)])]
+    for k, (start, end) in enumerate(CHUNKS):
+        copies.append(
+            pltpu.make_async_copy(signal.at[start:end], samples.at[start:end], sems.at[k])
+        )
+    for copy in copies:
+        copy.start()
+    fill_table(table)
+    copies[0].wait()
+    weights = usable[...].astype(jnp.float32)
+    arrives = {start: copy for (start, _), copy in zip(CHUNKS, copies[1:])}
+    for c0 in range(0, CH_DEV, 2):
+        if c0 in arrives:
+            arrives[c0].wait()
+        both = samples[c0 : c0 + 2].reshape(2 * LANES, SAMPLES)
         spec = lax.dot_general(
             table[...], both, (((1,), (1,)), ((), ())), preferred_element_type=jnp.float32
         )
         power = jnp.sum(spec * spec, axis=0, keepdims=True) * (1.0 / BINS)
         factor = lax.rsqrt(power + 1e-06)
         for one in range(2):
-            c = 2 * pair + one
             lanes = slice(one * LANES, (one + 1) * LANES)
-            scale = factor[:, lanes] * weights[c : c + 1, :]
-            white[c] = (spec[:, lanes] * scale).astype(jnp.bfloat16)
-    own_rows = pl.ds(pl.multiple_of(16 * g, 16), 16)
-    for h in range(2):
-        for r in range(2):
-            for m in range(3):
-                start = BINS * r + 96 * h + 32 * m
-                rows = jnp.swapaxes(white[:, start : start + 32, :], 0, 1)
-                if m == 2:
-                    out[:, g, h, r, 32:48, :] = rows
-                else:
-                    out[16 * m : 16 * m + 16, :, h, r, own_rows, :] = rows.reshape(16, 2, 16, LANES)
+            scale = factor[:, lanes] * weights[c0 + one : c0 + one + 1, :]
+            white[c0 + one] = (spec[:, lanes] * scale).astype(jnp.bfloat16)
 
 
 def whitened(signal, valid):
+    signal = pltpu.with_memory_space_constraint(signal, pltpu.HBM)
+    valid = pltpu.with_memory_space_constraint(valid, pltpu.HBM)
     return pl.pallas_call(
         whiten_kernel,
-        grid=(2,),
-        in_specs=[
-            pl.BlockSpec((16, LANES, SAMPLES), lambda g: (g, 0, 0)),
-            pl.BlockSpec((16, LANES), lambda g: (g, 0)),
+        in_specs=[pl.BlockSpec(memory_space=pltpu.HBM)] * 2,
+        out_specs=vmem(),
+        out_shape=jax.ShapeDtypeStruct((CH_DEV, 2 * BINS, LANES), jnp.bfloat16),
+        scratch_shapes=[
+            pltpu.VMEM((CH_DEV, LANES, SAMPLES), jnp.bfloat16),
+            pltpu.VMEM((CH_DEV, LANES), jnp.int32),
+            pltpu.VMEM((2 * BINS, SAMPLES), jnp.bfloat16),
+            pltpu.SemaphoreType.DMA((len(CHUNKS) + 1,)),
         ],
-        out_specs=vmem(),
-        out_shape=jax.ShapeDtypeStruct((32, 2, 2, 2, 48, LANES), jnp.bfloat16),
-        scratch_shapes=[
-            pltpu.VMEM((2 * BINS, SAMPLES), jnp.bfloat16),
-            pltpu.VMEM((16, 2 * BINS, LANES), jnp.bfloat16),
-        ],
-        compiler_params=limit(54),
+        compiler_params=limit(40),
         cost_estimate=pl.CostEstimate(
             flops=2 * 2 * BINS * SAMPLES * 4096, bytes_accessed=12 << 20, transcendentals=0
         ),
         name="whiten",
     )(signal, valid)
+
+
+def place_kernel(white, out):
+    for g in range(2):
+        c = slice(16 * g, 16 * g + 16)
+        for h in range(2):
+            for r in range(2):
+                for m in range(3):
+                    start = BINS * r + 96 * h + 32 * m
+                    rows = jnp.swapaxes(white[c, start : start + 32, :], 0, 1)
+                    if m == 2:
+                        out[:, g, h, r, 32:48, :] = rows
+                    else:
+                        to = slice(16 * m, 16 * m + 16)
+                        out[to, :, h, r, c, :] = rows.reshape(16, 2, 16, LANES)
+
+
+def placed(white):
+    return pl.pallas_call(
+        place_kernel,
+        in_specs=[vmem()],
+        out_specs=vmem(),
+        out_shape=jax.ShapeDtypeStruct((32, 2, 2, 2, 48, LANES), jnp.bfloat16),
+        compiler_params=limit(16),
+        cost_estimate=pl.CostEstimate(flops=0, bytes_accessed=6 << 20, transcendentals=0),
+        name="place",
+    )(white)
 
 
 def pick_kernel(owners, got, out):
@@ -237,7 +260,7 @@
 
 def per_device(signal, valid, owners):
     got = lax.all_to_all(
-        whitened(signal, valid).reshape(128, 2, 48, LANES), ("chan", "win"), 0, 0, tiled=True
+        placed(whitened(signal, valid)).reshape(128, 2, 48, LANES), ("chan", "win"), 0, 0, tiled=True
     ).reshape(N_CHAN, 2, 2, 48, LANES)
     own = picked(owners, got)
     other = lax.ppermute(own, "chan", [(i, i ^ 1) for i in range(N_CHAN)])

time: 93.5 us -> 89.8 us (0.960)
  Pallas kernels: 14.3 us -> 10.9 us
    pallas_call x1 -> x2, Pallas kernels: 10.3 us -> 6.84 us  [the longest x1 5.89 us: whitened(): pl.pallas_call(whiten_kernel, in_specs=[pl.BlockSpec(memory_space=pltpu.H...]
where the time goes in v3:
time: 89.8 us; the launch traced here: 89.7 us
  blocking collectives  77.7 us (87%)
  Pallas kernels  10.9 us (12%)
  starting transfers between devices  1.06 us (1%)
    all_to_all x1, blocking collectives, per_device(): lax.all_to_all(placed(whitened(signal, valid)).reshape(128, 2, 48, LANES)...  52.8 us
    all_to_all x1, blocking collectives, per_device(): back = lax.all_to_all(result, 'chan', 0, 0, tiled=True)  24.9 us
    pallas_call x1, Pallas kernels, whitened(): pl.pallas_call(whiten_kernel, in_specs=[pl.BlockSpec(memory_space=pltpu.H...  5.89 us
  transfers between devices with their start and end apart: 1, of which 0 were waited for; matrix products, arithmetic and copies ran while one was open for 0% of the time, Pallas kernels for 1%

profile of v3, /device:TPU:1, one launch (start us, length us, event | category | flops | bytes accessed | tf_op | source)
XLA Modules:
  0.0 89.7 jit_solution(16121881339497766340)
XLA Ops:
  0.0 5.9 %whiten.1.white = bf16[32,384,128]{2,1,0:T(8,128)(2,1)S(1)} custom-call(bf16[32,128,1024]{2,1,0:T(8,128)(2,1)} %signal.1, s32[32,128]{1,0:T(8,128)} %valid.1), custom_call_target="tpu_custom_call" | custom-call | flops 3221225472 | bytes 12582912 | tf_op jit(solution)/shard_map/whiten/pallas_call | solution.py:81
  5.9 0.9 %place.1 = bf16[32,2,2,2,48,128]{5,4,3,2,1,0:T(8,128)(2,1)S(1)} custom-call(bf16[32,384,128]{2,1,0:T(8,128)(2,1)S(1)} %whiten.1.white), custom_call_target="tpu_custom_call" | custom-call | bytes 6291456 | tf_op jit(solution)/shard_map/place/pallas_call | solution.py:116
  6.9 0.0 copy-start
  6.9 52.8 %all_to_all.10 = bf16[128,2,48,128]{3,2,1,0:T(8,128)(2,1)S(1)} all-to-all(bf16[128,2,48,128]{3,2,1,0:T(8,128)(2,1)S(1)} %bitcast.8), channel_id=1, replica_groups=mesh['chan'=64,'win'=2] {'chan','win'}, dimensions={0} | all-to-all | bytes 6291456 | tf_op jit(solution)/shard_map/all_to_all | solution.py:262
  59.7 0.0 copy-done
  59.7 0.5 pick.1.own
  60.3 1.1 %collective-permute-start = (bf16[3,2,2,16,128]{4,3,2,1,0:T(8,128)(2,1)S(1)}, bf16[3,2,2,16,128]{4,3,2,1,0:T(8,128)(2,1)S(1)}, u32[]{:S(2)}, u32[]{:S(2)}) collective-permute-start(bf16[3,2,2,16,128]{4,3,2,1,0:T(8,128)(2,1)S(1)} %pick.1.own), channel_id=1, source_target_pairs={{0,2},{2,0},{4,6},{6,4},{8,10},{10,8},{12,14},{14,12},{16,18},{18,... | collective-permute-start | bytes 147464 | tf_op jit(solution)/shard_map/ppermute | solution.py:266
  61.3 1.3 %cross_full.1.partial = bf16[64,72,128]{2,1,0:T(8,128)(2,1)S(1)} custom-call(s32[3]{0:T(128)S(1)} %copy-done, bf16[64,2,2,48,128]{4,3,2,1,0:T(8,128)(2,1)S(1)} %bitcast.6), custom_call_target="tpu_custom_call" | custom-call | flops 402653184 | bytes 3145728 | tf_op jit(solution)/shard_map/cross_full/pallas_call | solution.py:179
  62.7 0.0 collective-permute-done.other
  62.7 0.5 cross_mid.1
  63.2 24.9 %all_to_all.11 = bf16[64,72,128]{2,1,0:T(8,128)(2,1)S(1)} all-to-all(bf16[64,72,128]{2,1,0:T(8,128)(2,1)S(1)} %cross_mid.1), channel_id=1, replica_groups=mesh['chan'=64,'win'=2] {'chan'}, dimensions={0} | all-to-all | bytes 2359296 | tf_op jit(solution)/shard_map/all_to_all | solution.py:269
  88.1 1.6 %order.1 = bf16[2,3,32,32,96]{4,3,2,1,0:T(8,128)(2,1)} custom-call(bf16[32,2,72,128]{3,2,1,0:T(8,128)(2,1)S(1)} %bitcast.9), custom_call_target="tpu_custom_call" | custom-call | bytes 4194304 | tf_op jit(solution)/shard_map/order/pallas_call | solution.py:249
Async XLA Ops:
  6.9 52.9 %copy-start = (s32[3]{0:T(128)S(1)}, s32[3]{0:T(128)}, u32[]{:S(2)}) copy-start(s32[3]{0:T(128)} %owners.3) | copy-start | bytes 40
  60.3 2.4 %collective-permute-start = (bf16[3,2,2,16,128]{4,3,2,1,0:T(8,128)(2,1)S(1)}, bf16[3,2,2,16,128]{4,3,2,1,0:T(8,128)(2,1)S(1)}, u32[]{:S(2)}, u32[]{:S(2)}) collective-permute-start(bf16[3,2,2,16,128]{4,3,2,1,0:T(8,128)(2,1)S(1)} %pick.1.own), channel_id=1, source_target_pairs={{0,2},{2,0},{4,6},{6,4},{8,10},{10,8},{12,14},{14,12},{16,18},{18,... | collective-permute-start | bytes 147464 | tf_op jit(solution)/shard_map/ppermute | solution.py:266

commit v4 on v3

--- a/solution.py
+++ b/solution.py
@@ -124,27 +124,34 @@
     )(white)
 
 
-def pick_kernel(owners, got, out):
-    for s in range(STEPS):
-        out[s] = got[owners[s], :, :, 32:48, :]
-
-
-def picked(owners, got):
-    return pl.pallas_call(
-        pick_kernel,
-        in_specs=[pl.BlockSpec(memory_space=pltpu.SMEM), vmem()],
-        out_specs=vmem(),
-        out_shape=jax.ShapeDtypeStruct((STEPS, 2, 2, 16, LANES), jnp.bfloat16),
-        compiler_params=limit(16),
-        cost_estimate=pl.CostEstimate(flops=0, bytes_accessed=98304, transcendentals=0),
-        name="pick",
-    )(owners, got)
-
-
 def planned_columns(planned):
     real = [jnp.concatenate([b[0, 0], b[0, 1], b[1, 0], b[1, 1]], axis=1) for b in planned]
     imag = [jnp.concatenate([-b[0, 1], b[0, 0], -b[1, 1], b[1, 0]], axis=1) for b in planned]
     return jnp.concatenate(real + imag, axis=0)
+
+
+def pick_kernel(owners, got, own, columns):
+    planned = []
+    for s in range(STEPS):
+        owner = owners[s]
+        own[s] = got[owner, :, :, 32:48, :]
+        planned.append(got[owner, :, :, :32, :])
+    columns[...] = planned_columns(planned)
+
+
+def picked(owners, got):
+    return pl.pallas_call(
+        pick_kernel,
+        in_specs=[pl.BlockSpec(memory_space=pltpu.SMEM), vmem()],
+        out_specs=[vmem(), vmem()],
+        out_shape=[
+            jax.ShapeDtypeStruct((STEPS, 2, 2, 16, LANES), jnp.bfloat16),
+            jax.ShapeDtypeStruct((COLUMNS, 4 * LANES), jnp.bfloat16),
+        ],
+        compiler_params=limit(16),
+        cost_estimate=pl.CostEstimate(flops=0, bytes_accessed=98304, transcendentals=0),
+        name="pick",
+    )(owners, got)
 
 
 def products(left, columns):
@@ -168,31 +175,29 @@
     return jnp.concatenate(parts, axis=1).astype(jnp.bfloat16)
 
 
-def full_kernel(owners, got, out, columns):
-    columns[...] = planned_columns([got[owners[s], :, :, :32, :] for s in range(STEPS)])
+def full_kernel(got, columns, out):
     for start in range(0, N_CHAN, 8):
         left = got[start : start + 8, :, :, :32, :]
         out[start : start + 8, :FULL_ROWS, :] = packed(products(left, columns[...]))
 
 
-def cross_full(owners, got):
+def cross_full(got, columns):
     return pl.pallas_call(
         full_kernel,
-        in_specs=[pl.BlockSpec(memory_space=pltpu.SMEM), vmem()],
+        in_specs=[vmem(), vmem()],
         out_specs=vmem(),
         out_shape=jax.ShapeDtypeStruct((N_CHAN, ROWS, LANES), jnp.bfloat16),
-        scratch_shapes=[pltpu.VMEM((COLUMNS, 4 * LANES), jnp.bfloat16)],
         compiler_params=limit(16),
         cost_estimate=pl.CostEstimate(
             flops=2 * 2048 * 512 * 192, bytes_accessed=3 << 20, transcendentals=0
         ),
         name="cross_full",
-    )(owners, got)
-
-
-def mid_kernel(core, got, own, other, partial, out, columns):
+    )(got, columns)
+
+
+def mid_kernel(got, own, other, partial, out, columns):
     del partial
-    first = core[0] == 0
+    first = (lax.axis_index("chan") & 1) == 0
     planned = []
     for s in range(STEPS):
         mine, theirs = own[s], other[s]
@@ -204,20 +209,20 @@
         out[start : start + 16, FULL_ROWS:, :] = packed(products(left, columns[...]))
 
 
-def cross_mid(core, got, own, other, partial):
+def cross_mid(got, own, other, partial):
     return pl.pallas_call(
         mid_kernel,
-        in_specs=[pl.BlockSpec(memory_space=pltpu.SMEM)] + [vmem()] * 4,
+        in_specs=[vmem()] * 4,
         out_specs=vmem(),
         out_shape=jax.ShapeDtypeStruct((N_CHAN, ROWS, LANES), jnp.bfloat16),
         scratch_shapes=[pltpu.VMEM((COLUMNS, 4 * LANES), jnp.bfloat16)],
-        input_output_aliases={4: 0},
+        input_output_aliases={3: 0},
         compiler_params=limit(16),
         cost_estimate=pl.CostEstimate(
             flops=2 * 1024 * 512 * 192, bytes_accessed=2 << 20, transcendentals=0
         ),
         name="cross_mid",
-    )(core, got, own, other, partial)
+    )(got, own, other, partial)
 
 
 def order_kernel(back, out):
@@ -262,10 +267,9 @@
     got = lax.all_to_all(
         placed(whitened(signal, valid)).reshape(128, 2, 48, LANES), ("chan", "win"), 0, 0, tiled=True
     ).reshape(N_CHAN, 2, 2, 48, LANES)
-    own = picked(owners, got)
+    own, columns = picked(owners, got)
     other = lax.ppermute(own, "chan", [(i, i ^ 1) for i in range(N_CHAN)])
-    core = (lax.axis_index("chan") & 1).reshape(1)
-    result = cross_mid(core, got, own, other, cross_full(owners, got))
+    result = cross_mid(got, own, other, cross_full(got, columns))
     back = lax.all_to_all(result, "chan", 0, 0, tiled=True)
     return jnp.transpose(ordered(back), (0, 1, 4, 2, 3))
 

time: 89.8 us -> 89.6 us (level)
  transfers between devices with their start and end apart: 1 -> 1, of which waited for: 0 -> 1; matrix products, arithmetic and copies ran while one was open for 0% -> 0% of each run, Pallas kernels for 1% -> 1%
where the time goes in v4:
time: 89.6 us; the launch traced here: 89.5 us
  blocking collectives  77.9 us (87%)
  Pallas kernels  10.3 us (11%)
  starting transfers between devices  1.06 us (1%)
    all_to_all x1, blocking collectives, per_device(): lax.all_to_all(placed(whitened(signal, valid)).reshape(128, 2, 48, LANES)...  52.8 us
    all_to_all x1, blocking collectives, per_device(): back = lax.all_to_all(result, 'chan', 0, 0, tiled=True)  25.1 us
    pallas_call x1, Pallas kernels, whitened(): pl.pallas_call(whiten_kernel, in_specs=[pl.BlockSpec(memory_space=pltpu.H...  5.89 us
  transfers between devices with their start and end apart: 1, of which 1 were waited for; matrix products, arithmetic and copies ran while one was open for 0% of the time, Pallas kernels for 1%

profile of v4, /device:TPU:1, one launch (start us, length us, event | category | flops | bytes accessed | tf_op | source)
XLA Modules:
  0.0 89.5 jit_solution(13544755129232783178)
XLA Ops:
  0.0 5.9 %whiten.1.white = bf16[32,384,128]{2,1,0:T(8,128)(2,1)S(1)} custom-call(bf16[32,128,1024]{2,1,0:T(8,128)(2,1)} %signal.1, s32[32,128]{1,0:T(8,128)} %valid.1), custom_call_target="tpu_custom_call" | custom-call | flops 3221225472 | bytes 12582912 | tf_op jit(solution)/shard_map/whiten/pallas_call | solution.py:81
  5.9 0.9 %place.1 = bf16[32,2,2,2,48,128]{5,4,3,2,1,0:T(8,128)(2,1)S(1)} custom-call(bf16[32,384,128]{2,1,0:T(8,128)(2,1)S(1)} %whiten.1.white), custom_call_target="tpu_custom_call" | custom-call | bytes 6291456 | tf_op jit(solution)/shard_map/place/pallas_call | solution.py:116
  6.9 0.0 copy-start
  6.9 52.8 %all_to_all.10 = bf16[128,2,48,128]{3,2,1,0:T(8,128)(2,1)S(1)} all-to-all(bf16[128,2,48,128]{3,2,1,0:T(8,128)(2,1)S(1)} %bitcast.7), channel_id=1, replica_groups=mesh['chan'=64,'win'=2] {'chan','win'}, dimensions={0} | all-to-all | bytes 6291456 | tf_op jit(solution)/shard_map/all_to_all | solution.py:267
  59.7 0.0 copy-done
  59.7 0.6 pick.1
  60.3 1.1 %collective-permute-start = (bf16[3,2,2,16,128]{4,3,2,1,0:T(8,128)(2,1)S(1)}, bf16[3,2,2,16,128]{4,3,2,1,0:T(8,128)(2,1)S(1)}, u32[]{:S(2)}, u32[]{:S(2)}) collective-permute-start(bf16[3,2,2,16,128]{4,3,2,1,0:T(8,128)(2,1)S(1)} %get-tuple-element.7.own), channel_id=1, source_target_pairs={{0,2},{2,0},{4,6},{6,4},{8,10},{10,8},{12,14},{14,12},{16,18},{18,... | collective-permute-start | bytes 147464 | tf_op jit(solution)/shard_map/ppermute | solution.py:271
  61.3 0.8 cross_full.1.partial
  62.2 0.1 collective-permute-done.other
  62.2 0.5 cross_mid.1
  62.8 25.1 %all_to_all.11 = bf16[64,72,128]{2,1,0:T(8,128)(2,1)S(1)} all-to-all(bf16[64,72,128]{2,1,0:T(8,128)(2,1)S(1)} %cross_mid.1), channel_id=1, replica_groups=mesh['chan'=64,'win'=2] {'chan'}, dimensions={0} | all-to-all | bytes 2359296 | tf_op jit(solution)/shard_map/all_to_all | solution.py:273
  87.9 1.6 %order.1 = bf16[2,3,32,32,96]{4,3,2,1,0:T(8,128)(2,1)} custom-call(bf16[32,2,72,128]{3,2,1,0:T(8,128)(2,1)S(1)} %bitcast.8), custom_call_target="tpu_custom_call" | custom-call | bytes 4194304 | tf_op jit(solution)/shard_map/order/pallas_call | solution.py:254
Async XLA Ops:
  6.9 52.9 %copy-start = (s32[3]{0:T(128)S(1)}, s32[3]{0:T(128)}, u32[]{:S(2)}) copy-start(s32[3]{0:T(128)} %owners.1) | copy-start | bytes 40
  60.3 1.9 %collective-permute-start = (bf16[3,2,2,16,128]{4,3,2,1,0:T(8,128)(2,1)S(1)}, bf16[3,2,2,16,128]{4,3,2,1,0:T(8,128)(2,1)S(1)}, u32[]{:S(2)}, u32[]{:S(2)}) collective-permute-start(bf16[3,2,2,16,128]{4,3,2,1,0:T(8,128)(2,1)S(1)} %get-tuple-element.7.own), channel_id=1, source_target_pairs={{0,2},{2,0},{4,6},{6,4},{8,10},{10,8},{12,14},{14,12},{16,18},{18,... | collective-permute-start | bytes 147464 | tf_op jit(solution)/shard_map/ppermute | solution.py:271

commit v5 on v4

--- a/solution.py
+++ b/solution.py
@@ -5,6 +5,7 @@
 from jax import lax
 from jax.experimental import pallas as pl
 from jax.experimental.pallas import tpu as pltpu
+from jax.sharding import Mesh
 from jax.sharding import PartitionSpec as P
 
 SAMPLES = 1024
@@ -105,11 +106,11 @@
                 for m in range(3):
                     start = BINS * r + 96 * h + 32 * m
                     rows = jnp.swapaxes(white[c, start : start + 32, :], 0, 1)
+                    rows = rows.reshape(2, 16, 16, LANES)
                     if m == 2:
-                        out[:, g, h, r, 32:48, :] = rows
+                        out[:, h, g, :, r, 32:48, :] = rows
                     else:
-                        to = slice(16 * m, 16 * m + 16)
-                        out[to, :, h, r, c, :] = rows.reshape(16, 2, 16, LANES)
+                        out[m, h, :, :, r, c, :] = rows
 
 
 def placed(white):
@@ -117,7 +118,7 @@
         place_kernel,
         in_specs=[vmem()],
         out_specs=vmem(),
-        out_shape=jax.ShapeDtypeStruct((32, 2, 2, 2, 48, LANES), jnp.bfloat16),
+        out_shape=jax.ShapeDtypeStruct((2, 2, 2, 16, 2, 48, LANES), jnp.bfloat16),
         compiler_params=limit(16),
         cost_estimate=pl.CostEstimate(flops=0, bytes_accessed=6 << 20, transcendentals=0),
         name="place",
@@ -134,8 +135,11 @@
     planned = []
     for s in range(STEPS):
         owner = owners[s]
-        own[s] = got[owner, :, :, 32:48, :]
-        planned.append(got[owner, :, :, :32, :])
+        y, x = lax.shift_right_logical(owner, 4), lax.shift_right_logical(owner, 2) & 3
+        zh, core = lax.shift_right_logical(owner, 1) & 1, owner & 1
+        at = core * 16 + x * 4 + y
+        own[s] = got[zh, :, at, :, 32:48, :]
+        planned.append(got[zh, :, at, :, :32, :])
     columns[...] = planned_columns(planned)
 
 
@@ -155,9 +159,9 @@
 
 
 def products(left, columns):
-    count, channels = left.shape[0], left.shape[3]
+    count, channels = left.shape[1], left.shape[3]
     rows = jnp.concatenate(
-        [left[:, w, r].reshape(count * channels, LANES) for w in range(2) for r in range(2)], axis=1
+        [left[w, :, r].reshape(count * channels, LANES) for w in range(2) for r in range(2)], axis=1
     )
     result = lax.dot_general(
         rows, columns, (((1,), (1,)), ((), ())), preferred_element_type=jnp.float32
@@ -177,7 +181,8 @@
 
 def full_kernel(got, columns, out):
     for start in range(0, N_CHAN, 8):
-        left = got[start : start + 8, :, :, :32, :]
+        zh, at = divmod(start, 32)
+        left = got[zh, :, at : at + 8, :, :32, :]
         out[start : start + 8, :FULL_ROWS, :] = packed(products(left, columns[...]))
 
 
@@ -197,7 +202,7 @@
 
 def mid_kernel(got, own, other, partial, out, columns):
     del partial
-    first = (lax.axis_index("chan") & 1) == 0
+    first = lax.axis_index("core") == 0
     planned = []
     for s in range(STEPS):
         mine, theirs = own[s], other[s]
@@ -205,7 +210,8 @@
         planned.append(jnp.concatenate([low, high], axis=2))
     columns[...] = planned_columns(planned)
     for start in range(0, N_CHAN, 16):
-        left = got[start : start + 16, :, :, 32:48, :]
+        zh, at = divmod(start, 32)
+        left = got[zh, :, at : at + 16, :, 32:48, :]
         out[start : start + 16, FULL_ROWS:, :] = packed(products(left, columns[...]))
 
 
@@ -232,16 +238,17 @@
     def turned(full, mid):
         return jnp.concatenate([full, mid], axis=0).T
 
-    full = jnp.swapaxes(back[:, :, pl.ds(first, 16), :].reshape(N_CHAN, 16, LANES), 0, 1)
-    mid = jnp.swapaxes(back[:, g, 48:64, :], 0, 1)
+    full = jnp.swapaxes(back[:, :, :, pl.ds(first, 16), :].reshape(N_CHAN, 16, LANES), 0, 1)
+    mid = jnp.swapaxes(back[:, g, :, 48:64, :].reshape(32, 16, LANES), 0, 1)
     for c in range(16):
         columns = turned(full[c], mid[c])
         for u in range(4):
             out[u // STEPS, u % STEPS, c] = columns[32 * u : 32 * u + 32]
-    rest = back[:, :, 32:48, :].reshape(N_CHAN, 16, LANES).astype(jnp.float32)
+    rest = back[:, :, :, 32:48, :].reshape(N_CHAN, 16, LANES).astype(jnp.float32)
     rest = jnp.where(g == 0, rest[:, :8], rest[:, 8:])
     rest = jnp.swapaxes(rest, 0, 1).astype(jnp.bfloat16)
-    mid = jnp.swapaxes(back[:, g, 64:72, :].astype(jnp.float32), 0, 1).astype(jnp.bfloat16)
+    mid = back[:, g, :, 64:72, :].astype(jnp.float32).reshape(32, 8, LANES)
+    mid = jnp.swapaxes(mid, 0, 1).astype(jnp.bfloat16)
     for e in range(8):
         columns = turned(rest[e], mid[e])
         for half in range(2):
@@ -260,23 +267,25 @@
         compiler_params=limit(24),
         cost_estimate=pl.CostEstimate(flops=0, bytes_accessed=4 << 20, transcendentals=0),
         name="order",
-    )(back.reshape(32, 2, ROWS, LANES))
+    )(back.reshape(2, 2, 16, ROWS, LANES))
 
 
 def per_device(signal, valid, owners):
-    got = lax.all_to_all(
-        placed(whitened(signal, valid)).reshape(128, 2, 48, LANES), ("chan", "win"), 0, 0, tiled=True
-    ).reshape(N_CHAN, 2, 2, 48, LANES)
+    chunks = placed(whitened(signal, valid)).reshape(128, 2, 48, LANES)
+    got = lax.all_to_all(chunks, ("zh", "zl", "core", "x", "y"), 0, 0, tiled=True)
+    got = got.reshape(2, 2, 32, 2, 48, LANES)
     own, columns = picked(owners, got)
-    other = lax.ppermute(own, "chan", [(i, i ^ 1) for i in range(N_CHAN)])
+    other = lax.ppermute(own, "core", [(0, 1), (1, 0)])
     result = cross_mid(got, own, other, cross_full(got, columns))
-    back = lax.all_to_all(result, "chan", 0, 0, tiled=True)
+    back = lax.all_to_all(result, ("zh", "core", "x", "y"), 0, 0, tiled=True)
     return jnp.transpose(ordered(back), (0, 1, 4, 2, 3))
 
 
 def solution(mesh):
-    in_specs = (P("chan", "win", None), P("chan", "win"), P())
-    out_specs = P(None, None, "win", "chan", None)
+    chan = ("y", "x", "zh", "core")
+    fine = Mesh(mesh.devices.reshape(4, 4, 2, 2, 2), chan + ("zl",))
+    in_specs = (P(chan, "zl", None), P(chan, "zl"), P())
+    out_specs = P(None, None, "zl", chan, None)
     return jax.shard_map(
-        per_device, mesh=mesh, in_specs=in_specs, out_specs=out_specs, check_vma=False
+        per_device, mesh=fine, in_specs=in_specs, out_specs=out_specs, check_vma=False
     )

time: 89.6 us -> 88.1 us (0.983)
  blocking collectives: 77.9 us -> 76.8 us
    all_to_all x2, blocking collectives: 77.9 us -> 76.8 us  [the longest x1 52.3 us: per_device(): lax.all_to_all(chunks, ('zh', 'zl', 'core', 'x', 'y'), 0, 0, tiled=True)]
where the time goes in v5:
time: 88.1 us; the launch traced here: 87.8 us
  blocking collectives  76.8 us (87%)
  Pallas kernels  10.4 us (12%)
    all_to_all x1, blocking collectives, per_device(): lax.all_to_all(chunks, ('zh', 'zl', 'core', 'x', 'y'), 0, 0, tiled=True)  52.3 us
    all_to_all x1, blocking collectives, per_device(): back = lax.all_to_all(result, ('zh', 'core', 'x', 'y'), 0, 0, tiled=True)  24.4 us
    pallas_call x1, Pallas kernels, whitened(): pl.pallas_call(whiten_kernel, in_specs=[pl.BlockSpec(memory_space=pltpu.H...  5.89 us
  transfers between devices with their start and end apart: 1, of which 1 were waited for; matrix products, arithmetic and copies ran while one was open for 0% of the time, Pallas kernels for 1%

profile of v5, /device:TPU:1, one launch (start us, length us, event | category | flops | bytes accessed | tf_op | source)
XLA Modules:
  0.0 87.8 jit_solution(13573799227607229346)
XLA Ops:
  0.0 5.9 %whiten.1.white = bf16[32,384,128]{2,1,0:T(8,128)(2,1)S(1)} custom-call(bf16[32,128,1024]{2,1,0:T(8,128)(2,1)} %signal.1, s32[32,128]{1,0:T(8,128)} %valid.1), custom_call_target="tpu_custom_call" | custom-call | flops 3221225472 | bytes 12582912 | tf_op jit(solution)/shard_map/whiten/pallas_call | solution.py:82
  5.9 0.9 %place.1 = bf16[2,2,2,16,2,48,128]{6,5,4,3,2,1,0:T(8,128)(2,1)S(1)} custom-call(bf16[32,384,128]{2,1,0:T(8,128)(2,1)S(1)} %whiten.1.white), custom_call_target="tpu_custom_call" | custom-call | bytes 6291456 | tf_op jit(solution)/shard_map/place/pallas_call | solution.py:117
  6.9 0.0 copy-start
  6.9 52.3 %all_to_all.10 = bf16[128,2,48,128]{3,2,1,0:T(8,128)(2,1)S(1)} all-to-all(bf16[128,2,48,128]{3,2,1,0:T(8,128)(2,1)S(1)} %bitcast.7), channel_id=1, replica_groups=mesh['y'=4,'x'=4,'zh'=2,'core'=2,'zl'=2] {'zh','zl','core','x','y'}, dimensions={0} | all-to-all | bytes 6291456 | tf_op jit(solution)/shard_map/all_to_all | solution.py:275
  59.2 0.0 copy-done
  59.2 0.6 pick.1
  59.8 0.6 collective-permute-start
  60.4 0.8 cross_full.1.partial
  61.2 0.1 collective-permute-done.other
  61.3 0.5 cross_mid.1
  61.8 24.4 %all_to_all.11 = bf16[64,72,128]{2,1,0:T(8,128)(2,1)S(1)} all-to-all(bf16[64,72,128]{2,1,0:T(8,128)(2,1)S(1)} %cross_mid.1), channel_id=1, replica_groups=mesh['y'=4,'x'=4,'zh'=2,'core'=2,'zl'=2] {'zh','core','x','y'}, dimensions={0} | all-to-all | bytes 2359296 | tf_op jit(solution)/shard_map/all_to_all | solution.py:280
  86.2 1.6 %order.1 = bf16[2,3,32,32,96]{4,3,2,1,0:T(8,128)(2,1)} custom-call(bf16[2,2,16,72,128]{4,3,2,1,0:T(8,128)(2,1)S(1)} %bitcast.8), custom_call_target="tpu_custom_call" | custom-call | bytes 4194304 | tf_op jit(solution)/shard_map/order/pallas_call | solution.py:261
Async XLA Ops:
  6.9 52.4 %copy-start = (s32[3]{0:T(128)S(1)}, s32[3]{0:T(128)}, u32[]{:S(2)}) copy-start(s32[3]{0:T(128)} %owners.1) | copy-start | bytes 40
  59.8 1.5 %collective-permute-start = (bf16[3,2,2,16,128]{4,3,2,1,0:T(8,128)(2,1)S(1)}, bf16[3,2,2,16,128]{4,3,2,1,0:T(8,128)(2,1)S(1)}, u32[]{:S(2)}, u32[]{:S(2)}) collective-permute-start(bf16[3,2,2,16,128]{4,3,2,1,0:T(8,128)(2,1)S(1)} %get-tuple-element.7.own), channel_id=1, source_target_pairs={{0,2},{2,0},{1,3},{3,1},{4,6},{6,4},{5,7},{7,5},{8,10},{10,8},{9,1... | collective-permute-start | bytes 147464 | tf_op jit(solution)/shard_map/ppermute | solution.py:278

commit v6 on v5

--- a/solution.py
+++ b/solution.py
@@ -17,7 +17,7 @@
 LANES = 128
 COLUMNS = 2 * STEPS * CH_DEV
 FULL_ROWS, ROWS = 48, 72
-CHUNKS = ((0, 4), (4, 12), (12, 32))
+CHUNKS = ((0, 8), (8, 20), (20, 32))
 
 
 def vmem():
@@ -55,7 +55,7 @@
         copies.append(
             pltpu.make_async_copy(signal.at[start:end], samples.at[start:end], sems.at[k])
         )
-    for copy in copies:
+    for copy in copies[:3]:
         copy.start()
     fill_table(table)
     copies[0].wait()
@@ -64,6 +64,8 @@
     for c0 in range(0, CH_DEV, 2):
         if c0 in arrives:
             arrives[c0].wait()
+            if c0 == 0:
+                copies[3].start()
         both = samples[c0 : c0 + 2].reshape(2 * LANES, SAMPLES)
         spec = lax.dot_general(
             table[...], both, (((1,), (1,)), ((), ())), preferred_element_type=jnp.float32
@@ -134,7 +136,7 @@
 def pick_kernel(owners, got, own, columns):
     planned = []
     for s in range(STEPS):
-        owner = owners[s]
+        owner = owners[0, s]
         y, x = lax.shift_right_logical(owner, 4), lax.shift_right_logical(owner, 2) & 3
         zh, core = lax.shift_right_logical(owner, 1) & 1, owner & 1
         at = core * 16 + x * 4 + y
@@ -146,7 +148,7 @@
 def picked(owners, got):
     return pl.pallas_call(
         pick_kernel,
-        in_specs=[pl.BlockSpec(memory_space=pltpu.SMEM), vmem()],
+        in_specs=[vmem(), vmem()],
         out_specs=[vmem(), vmem()],
         out_shape=[
             jax.ShapeDtypeStruct((STEPS, 2, 2, 16, LANES), jnp.bfloat16),
@@ -155,7 +157,7 @@
         compiler_params=limit(16),
         cost_estimate=pl.CostEstimate(flops=0, bytes_accessed=98304, transcendentals=0),
         name="pick",
-    )(owners, got)
+    )(owners.reshape(1, STEPS), got)
 
 
 def products(left, columns):
@@ -231,39 +233,52 @@
     )(got, own, other, partial)
 
 
-def order_kernel(back, out):
-    g = pl.program_id(0)
-    first = pl.multiple_of(16 * g, 16)
+def order_kernel(back, out, held, sems):
+    copies = []
+
+    def send(real, steps, channels):
+        part = (real, steps, channels)
+        copies.append(pltpu.make_async_copy(held.at[part], out.at[part], sems.at[len(copies)]))
+        copies[-1].start()
 
     def turned(full, mid):
         return jnp.concatenate([full, mid], axis=0).T
 
-    full = jnp.swapaxes(back[:, :, :, pl.ds(first, 16), :].reshape(N_CHAN, 16, LANES), 0, 1)
-    mid = jnp.swapaxes(back[:, g, :, 48:64, :].reshape(32, 16, LANES), 0, 1)
-    for c in range(16):
-        columns = turned(full[c], mid[c])
-        for u in range(4):
-            out[u // STEPS, u % STEPS, c] = columns[32 * u : 32 * u + 32]
-    rest = back[:, :, :, 32:48, :].reshape(N_CHAN, 16, LANES).astype(jnp.float32)
-    rest = jnp.where(g == 0, rest[:, :8], rest[:, 8:])
-    rest = jnp.swapaxes(rest, 0, 1).astype(jnp.bfloat16)
-    mid = back[:, g, :, 64:72, :].astype(jnp.float32).reshape(32, 8, LANES)
-    mid = jnp.swapaxes(mid, 0, 1).astype(jnp.bfloat16)
-    for e in range(8):
-        columns = turned(rest[e], mid[e])
-        for half in range(2):
-            for u in (4, 5):
-                start = 64 * half + 32 * (u - 4)
-                out[u // STEPS, u % STEPS, e + 8 * half] = columns[start : start + 32]
+    for g in range(2):
+        first, packed_row = 16 * g, 32 + 8 * g
+        channels = slice(first, first + 16)
+        full = jnp.swapaxes(back[:, :, :, channels, :].reshape(N_CHAN, 16, LANES), 0, 1)
+        mid = jnp.swapaxes(back[:, g, :, 48:64, :].reshape(32, 16, LANES), 0, 1)
+        for c in range(16):
+            columns = turned(full[c], mid[c])
+            for u in range(4):
+                held[u // STEPS, u % STEPS, first + c] = columns[32 * u : 32 * u + 32]
+        send(0, slice(0, STEPS), channels)
+        send(1, slice(0, 1), channels)
+        rest = back[:, :, :, packed_row : packed_row + 8, :].astype(jnp.float32)
+        rest = jnp.swapaxes(rest.reshape(N_CHAN, 8, LANES), 0, 1).astype(jnp.bfloat16)
+        mid = back[:, g, :, 64:72, :].astype(jnp.float32).reshape(32, 8, LANES)
+        mid = jnp.swapaxes(mid, 0, 1).astype(jnp.bfloat16)
+        for e in range(8):
+            columns = turned(rest[e], mid[e])
+            for half in range(2):
+                for u in (4, 5):
+                    start = 64 * half + 32 * (u - 4)
+                    at = first + e + 8 * half
+                    held[u // STEPS, u % STEPS, at] = columns[start : start + 32]
+        send(1, slice(1, STEPS), channels)
+    for copy in copies:
+        copy.wait()
 
 
 def ordered(back):
+    shape = (2, STEPS, 32, 32, 96)
     return pl.pallas_call(
         order_kernel,
-        grid=(2,),
         in_specs=[vmem()],
-        out_specs=pl.BlockSpec((2, STEPS, 16, 32, 96), lambda g: (0, 0, g, 0, 0)),
-        out_shape=jax.ShapeDtypeStruct((2, STEPS, 32, 32, 96), jnp.bfloat16),
+        out_specs=pl.BlockSpec(memory_space=pl.ANY),
+        out_shape=jax.ShapeDtypeStruct(shape, jnp.bfloat16),
+        scratch_shapes=[pltpu.VMEM(shape, jnp.bfloat16), pltpu.SemaphoreType.DMA((6,))],
         compiler_params=limit(24),
         cost_estimate=pl.CostEstimate(flops=0, bytes_accessed=4 << 20, transcendentals=0),
         name="order",

time: 88.1 us -> 87.4 us (level)
  no operation moved by 1% of the time
where the time goes in v6:
time: 87.4 us; the launch traced here: 87.2 us
  blocking collectives  76.8 us (88%)
  Pallas kernels  9.7 us (11%)
    all_to_all x1, blocking collectives, per_device(): lax.all_to_all(chunks, ('zh', 'zl', 'core', 'x', 'y'), 0, 0, tiled=True)  52.3 us
    all_to_all x1, blocking collectives, per_device(): back = lax.all_to_all(result, ('zh', 'core', 'x', 'y'), 0, 0, tiled=True)  24.4 us
    pallas_call x1, Pallas kernels, whitened(): pl.pallas_call(whiten_kernel, in_specs=[pl.BlockSpec(memory_space=pltpu.H...  5.8 us
  transfers between devices with their start and end apart: 1, of which 1 were waited for; matrix products, arithmetic and copies ran while one was open for 0% of the time, Pallas kernels for 1%

profile of v6, /device:TPU:1, one launch (start us, length us, event | category | flops | bytes accessed | tf_op | source)
XLA Modules:
  0.0 87.2 jit_solution(4867125531191037426)
XLA Ops:
  0.0 5.8 %whiten.1.white = bf16[32,384,128]{2,1,0:T(8,128)(2,1)S(1)} custom-call(bf16[32,128,1024]{2,1,0:T(8,128)(2,1)} %signal.1, s32[32,128]{1,0:T(8,128)} %valid.1), custom_call_target="tpu_custom_call" | custom-call | flops 3221225472 | bytes 12582912 | tf_op jit(solution)/shard_map/whiten/pallas_call | solution.py:84
  5.8 0.9 %place.1 = bf16[2,2,2,16,2,48,128]{6,5,4,3,2,1,0:T(8,128)(2,1)S(1)} custom-call(bf16[32,384,128]{2,1,0:T(8,128)(2,1)S(1)} %whiten.1.white), custom_call_target="tpu_custom_call" | custom-call | bytes 6291456 | tf_op jit(solution)/shard_map/place/pallas_call | solution.py:119
  6.8 0.0 copy-start
  6.8 52.3 %all_to_all.10 = bf16[128,2,48,128]{3,2,1,0:T(8,128)(2,1)S(1)} all-to-all(bf16[128,2,48,128]{3,2,1,0:T(8,128)(2,1)S(1)} %bitcast.8), channel_id=1, replica_groups=mesh['y'=4,'x'=4,'zh'=2,'core'=2,'zl'=2] {'zh','zl','core','x','y'}, dimensions={0} | all-to-all | bytes 6291456 | tf_op jit(solution)/shard_map/all_to_all | solution.py:290
  59.1 0.0 copy-done
  59.1 0.1 pick.1
  59.3 0.6 collective-permute-start
  59.8 0.8 cross_full.1.partial
  60.7 0.1 collective-permute-done.other
  60.7 0.5 cross_mid.1
  61.3 24.4 %all_to_all.11 = bf16[64,72,128]{2,1,0:T(8,128)(2,1)S(1)} all-to-all(bf16[64,72,128]{2,1,0:T(8,128)(2,1)S(1)} %cross_mid.1), channel_id=1, replica_groups=mesh['y'=4,'x'=4,'zh'=2,'core'=2,'zl'=2] {'zh','core','x','y'}, dimensions={0} | all-to-all | bytes 2359296 | tf_op jit(solution)/shard_map/all_to_all | solution.py:295
  85.7 1.5 %order.1 = bf16[2,3,32,32,96]{4,3,2,1,0:T(8,128)(2,1)} custom-call(bf16[2,2,16,72,128]{4,3,2,1,0:T(8,128)(2,1)S(1)} %bitcast.9), custom_call_target="tpu_custom_call" | custom-call | bytes 4194304 | tf_op jit(solution)/shard_map/order/pallas_call | solution.py:276
Async XLA Ops:
  6.8 52.4 %copy-start = (s32[3]{0:T(128)S(1)}, s32[3]{0:T(128)}, u32[]{:S(2)}) copy-start(s32[3]{0:T(128)} %param.5) | copy-start | bytes 40
  59.3 1.5 %collective-permute-start = (bf16[3,2,2,16,128]{4,3,2,1,0:T(8,128)(2,1)S(1)}, bf16[3,2,2,16,128]{4,3,2,1,0:T(8,128)(2,1)S(1)}, u32[]{:S(2)}, u32[]{:S(2)}) collective-permute-start(bf16[3,2,2,16,128]{4,3,2,1,0:T(8,128)(2,1)S(1)} %get-tuple-element.7.own), channel_id=1, source_target_pairs={{0,2},{2,0},{1,3},{3,1},{4,6},{6,4},{5,7},{7,5},{8,10},{10,8},{9,1... | collective-permute-start | bytes 147464 | tf_op jit(solution)/shard_map/ppermute | solution.py:293
